TPU v7x, 32 devices: a whole 2x2x4 slice. The times are simulated.
32 devices in a mesh: row: 4 (over z), col: 8 (over y, x, core).
Axes of the slice: x: 2, y: 2, z: 4, core: 2. Of those that a mesh axis runs over, the one named last changes fastest.
Arguments:
- queries: bfloat16 [4, 1024, 512], P('row', 'col'), may hold values from -6 to 6
- keys: bfloat16 [8, 512, 512], P('col', 'row'), may hold values from -6 to 6
- values: bfloat16 [8, 512, 512], P('col', 'row'), may hold values from -6 to 6
- outputs: bfloat16 [4, 1024, 512], P('row', 'col'), may hold values from -2 to 2
- grad_out: bfloat16 [4, 1024, 512], P('row', 'col'), may hold values from -48 to 48
- lse: float32 [4, 8, 1024], P('row'), may hold values from 7 to 9.5
- tile_slot: int32 [4, 8, 24], P('row', 'col'), may hold values from 0 to 31, as said below
- tile_live: int32 [4, 8], P('row', 'col'), may hold values from 1 to 24, as said below
- tile_bits: int32 [4, 8, 24, 8, 128], P('row', 'col'), may hold values from 0 to 65535, as said below
Outputs:
- grad_queries: bfloat16 [4, 1024, 512], P('row', 'col')
- grad_keys: bfloat16 [8, 512, 512], P('col', 'row')
- grad_values: bfloat16 [8, 512, 512], P('col', 'row')
Inputs may be any that keep to these rules, and one draw needn't show every extreme that they name: `tile_slot`: the 24 entries of one pair of blocks are distinct slots. `tile_live`: some pair of blocks has all 24 entries live. `tile_bits`: each word holds 16 edge bits in its low bits.
All inputs are finite; a program needn't handle non-finite values.
Results may differ from a plain program's by a relative error of at most 0.02.
Values may be sent and summed in bfloat16 or wider, within the bound.
No kernel may reach another device: no remote copies, remote signals or barrier semaphores. Data moves between devices by JAX's collectives and lax.ppermute only.
A program may use at most 64 MiB of HBM per device.

v0:
```python
import jax
import jax.numpy as jnp
from jax import lax
from jax.sharding import PartitionSpec as P


def unpack_bits(packed_rows):
    shifts = jnp.arange(16, dtype=jnp.int32)
    bit_values = jnp.bitwise_and(jnp.right_shift(packed_rows[:, :, None], shifts), 1)
    return (
        jnp.transpose(bit_values, (1, 0, 2)).reshape(
            packed_rows.shape[1], packed_rows.shape[0] * 16
        )
        == 1
    )


def row_delta(grads, outs, head_count):
    leading = grads.shape[:-1]
    model_width = grads.shape[-1]
    product = (grads.astype(jnp.float32) * outs.astype(jnp.float32)).reshape(
        leading + (head_count, model_width // head_count)
    )
    return jnp.swapaxes(jnp.sum(product, axis=-1), -1, -2).astype(jnp.bfloat16)


def add_rows(total, piece, start):
    current = lax.dynamic_slice_in_dim(total, start, piece.shape[0], 0)
    return lax.dynamic_update_slice_in_dim(total, current + piece, start, 0)


def body(queries, keys, values, outputs, grad_out, lse, tile_slot, tile_live, tile_bits):
    head_count = lse.shape[1]
    model_width = queries.shape[2]
    head_dim = model_width // head_count
    tile_size = tile_bits.shape[4]
    scaling = float(head_dim) ** (-0.5)
    query_all, grad_all, out_all = (
        lax.all_gather(queries, "col", axis=1, tiled=True),
        lax.all_gather(grad_out, "col", axis=1, tiled=True),
        lax.all_gather(outputs, "col", axis=1, tiled=True),
    )
    delta_rows = row_delta(grad_all, out_all, head_count)[0]
    key_all, value_all = (
        lax.all_gather(keys, "row", axis=1, tiled=True),
        lax.all_gather(values, "row", axis=1, tiled=True),
    )
    query_block = query_all[0]
    grad_block = grad_all[0]
    key_block = key_all[0]
    value_block = value_all[0]
    lse_rows = lse[0]
    slot_list = tile_slot[0, 0]
    live_count = tile_live[0, 0]
    packed = tile_bits[0, 0]
    key_tiles = key_block.shape[0] // tile_size

    def starts_of(slot_index):
        slot_value = slot_list[slot_index]
        return (slot_value // key_tiles * tile_size, slot_value % key_tiles * tile_size)

    def key_tile_of(k_start):
        return lax.dynamic_slice_in_dim(key_block, k_start, tile_size, 0).reshape(
            tile_size, head_count, head_dim
        )

    def tile_core(slot_index):
        q_start, k_start = starts_of(slot_index)
        q_tile = lax.dynamic_slice_in_dim(query_block, q_start, tile_size, 0).reshape(
            tile_size, head_count, head_dim
        )
        g_tile = lax.dynamic_slice_in_dim(grad_block, q_start, tile_size, 0).reshape(
            tile_size, head_count, head_dim
        )
        k_tile = key_tile_of(k_start)
        v_tile = lax.dynamic_slice_in_dim(value_block, k_start, tile_size, 0).reshape(
            tile_size, head_count, head_dim
        )
        lse_tile = lax.dynamic_slice_in_dim(lse_rows, q_start, tile_size, 1)
        delta_tile = lax.dynamic_slice_in_dim(delta_rows, q_start, tile_size, 1).astype(jnp.float32)
        edge_mask = jnp.logical_and(unpack_bits(packed[slot_index]), slot_index < live_count)
        scores = (
            jnp.einsum("ihd,jhd->hij", q_tile, k_tile, preferred_element_type=jnp.float32) * scaling
        )
        attn_prob = jnp.where(edge_mask[None], jnp.exp(scores - lse_tile[:, :, None]), 0.0)
        prob_low = attn_prob.astype(jnp.bfloat16)
        value_tile_grad = jnp.einsum(
            "hij,ihd->jhd", prob_low, g_tile, preferred_element_type=jnp.float32
        ).reshape(tile_size, model_width)
        grad_prob = jnp.einsum("ihd,jhd->hij", g_tile, v_tile, preferred_element_type=jnp.float32)
        score_low = (attn_prob * (grad_prob - delta_tile[:, :, None])).astype(jnp.bfloat16)
        key_tile_grad = (
            jnp.einsum(
                "hij,ihd->jhd", score_low, q_tile, preferred_element_type=jnp.float32
            ).reshape(tile_size, model_width)
            * scaling
        )
        return (q_start, k_start, k_tile, score_low, key_tile_grad, value_tile_grad)

    def query_piece(score_low, k_tile):
        return (
            jnp.einsum(
                "hij,jhd->ihd", score_low, k_tile, preferred_element_type=jnp.float32
            ).reshape(tile_size, model_width)
            * scaling
        )

    limit = packed.shape[0]
    key_zeros = jnp.zeros(key_block.shape, jnp.float32)

    def one_tile(slot_index, running):
        grad_q, grad_k, grad_v = running
        q_start, k_start, k_tile, score_low, key_tile_grad, value_tile_grad = tile_core(slot_index)
        grad_q = add_rows(grad_q, query_piece(score_low, k_tile), q_start)
        grad_k = add_rows(grad_k, key_tile_grad, k_start)
        grad_v = add_rows(grad_v, value_tile_grad, k_start)
        return (grad_q, grad_k, grad_v)

    start_sums = (jnp.zeros(query_block.shape, jnp.float32), key_zeros, key_zeros)
    grad_q, grad_k, grad_v = lax.fori_loop(0, limit, one_tile, start_sums)
    query_grad_sum = lax.psum_scatter(
        grad_q[None].astype(jnp.bfloat16), "col", scatter_dimension=1, tiled=True
    )
    key_grad_sum, value_grad_sum = (
        lax.psum_scatter(
            grad_k[None].astype(jnp.bfloat16), "row", scatter_dimension=1, tiled=True
        ).astype(jnp.float32),
        lax.psum_scatter(
            grad_v[None].astype(jnp.bfloat16), "row", scatter_dimension=1, tiled=True
        ).astype(jnp.float32),
    )
    return (query_grad_sum, key_grad_sum.astype(jnp.bfloat16), value_grad_sum.astype(jnp.bfloat16))


def solution(mesh):
    in_specs = (
        P("row", "col", None),
        P("col", "row", None),
        P("col", "row", None),
        P("row", "col", None),
        P("row", "col", None),
        P("row", None, None),
        P("row", "col", None),
        P("row", "col"),
        P("row", "col", None, None, None),
    )
    out_specs = (P("row", "col", None), P("col", "row", None), P("col", "row", None))
    return jax.shard_map(body, mesh=mesh, in_specs=in_specs, out_specs=out_specs, check_vma=False)
```

profile of v0, /device:TPU:0, one launch (start us, length us, event | category | flops | bytes accessed | tf_op | source)
XLA Modules:
  0.0 541.3 jit_solution(15823061989430172637)
XLA Ops:
  7.2 1.7 copy.26
  8.9 1.7 copy.24
  10.7 1.7 copy.23
  12.4 1.0 copy.22
  13.5 1.0 copy.25
  14.5 17.1 %all_gather.18 = bf16[1,512,512]{1,2,0:T(8,128)(2,1)} all-gather(bf16[1,128,512]{1,2,0:T(8,128)(2,1)S(1)} %copy.25), channel_id=1, replica_groups=mesh['row'=4,'col'=8] {'row'}, dimensions={1}, use_global_device_ids=true | all-gather | bytes 655360 | tf_op jit(solution)/shard_map/all_gather | solution.py:46
  31.6 15.4 %all_gather.15 = bf16[1,512,512]{1,2,0:T(8,128)(2,1)} all-gather(bf16[1,128,512]{1,2,0:T(8,128)(2,1)S(1)} %copy.22), channel_id=1, replica_groups=mesh['row'=4,'col'=8] {'row'}, dimensions={1}, use_global_device_ids=true | all-gather | bytes 655360 | tf_op jit(solution)/shard_map/all_gather | solution.py:45
  47.0 15.8 %all-gather.6.cloned.1.call-done = bf16[1,1024,512]{1,2,0:T(8,128)(2,1)} async-done(((bf16[1,128,512]{1,2,0:T(8,128)(2,1)}), bf16[1,1024,512]{1,2,0:T(8,128)(2,1)}) %all-gather.6.cloned.1.call-update) | async-done | bytes 1048592 | tf_op jit(solution)/shard_map/all_gather | solution.py:40
  62.8 1.9 convert_multiply_fusion
  65.0 23.9 %all-gather.4.cloned.1.call-done = bf16[1,1024,512]{1,2,0:T(8,128)(2,1)} async-done(((bf16[1,128,512]{1,2,0:T(8,128)(2,1)}), bf16[1,1024,512]{1,2,0:T(8,128)(2,1)}) %all-gather.4.cloned.1.call-update) | async-done | bytes 1048592 | tf_op jit(solution)/shard_map/all_gather | solution.py:39
  89.0 1.1 broadcast_in_dim.55.clone
  90.1 1.6 broadcast_in_dim.54.clone
  91.7 359.4 %while.19 = (s32[]{:T(128)}, f32[1024,512]{1,0:T(8,128)}, f32[512,512]{1,0:T(8,128)}, f32[512,512]{1,0:T(8,128)S(1)}, s32[24]{0:T(128)S(1)}, /*index=5*/bf16[512...) while((s32[]{:T(128)}, f32[1024,512]{1,0:T(8,128)}, ...), condition=%wide.region_2.3_spmd, body=%wide.region_1.2_spmd.sunk | while | flops 85197856 | bytes 13865514 | solution.py:120
  100.9 1.0 constant_dynamic-slice_fusion.17
  102.1 1.0 constant_dynamic-slice_fusion.24
  115.9 1.0 constant_dynamic-slice_fusion.17
  117.0 1.0 constant_dynamic-slice_fusion.24
  130.9 1.0 constant_dynamic-slice_fusion.17
  132.0 1.0 constant_dynamic-slice_fusion.24
  145.9 1.0 constant_dynamic-slice_fusion.17
  147.0 1.0 constant_dynamic-slice_fusion.24
  160.8 1.0 constant_dynamic-slice_fusion.17
  161.9 1.0 constant_dynamic-slice_fusion.24
  175.8 1.0 constant_dynamic-slice_fusion.17
  176.9 1.0 constant_dynamic-slice_fusion.24
  190.8 1.0 constant_dynamic-slice_fusion.17
  191.9 1.0 constant_dynamic-slice_fusion.24
  205.7 1.0 constant_dynamic-slice_fusion.17
  206.8 1.0 constant_dynamic-slice_fusion.24
  220.7 1.0 constant_dynamic-slice_fusion.17
  221.8 1.0 constant_dynamic-slice_fusion.24
  235.7 1.0 constant_dynamic-slice_fusion.17
  236.8 1.0 constant_dynamic-slice_fusion.24
  250.7 1.0 constant_dynamic-slice_fusion.17
  251.8 1.0 constant_dynamic-slice_fusion.24
  265.6 1.0 constant_dynamic-slice_fusion.17
  266.8 1.0 constant_dynamic-slice_fusion.24
  280.6 1.0 constant_dynamic-slice_fusion.17
  281.7 1.0 constant_dynamic-slice_fusion.24
  295.6 1.0 constant_dynamic-slice_fusion.17
  296.7 1.0 constant_dynamic-slice_fusion.24
  310.6 1.0 constant_dynamic-slice_fusion.17
  311.7 1.0 constant_dynamic-slice_fusion.24
  325.6 1.0 constant_dynamic-slice_fusion.17
  326.7 1.0 constant_dynamic-slice_fusion.24
  340.5 1.0 constant_dynamic-slice_fusion.17
  341.6 1.0 constant_dynamic-slice_fusion.24
  355.5 1.0 constant_dynamic-slice_fusion.17
  356.6 1.0 constant_dynamic-slice_fusion.24
  370.5 1.0 constant_dynamic-slice_fusion.17
  371.6 1.0 constant_dynamic-slice_fusion.24
  385.5 1.0 constant_dynamic-slice_fusion.17
  386.6 1.0 constant_dynamic-slice_fusion.24
  400.4 1.0 constant_dynamic-slice_fusion.17
  401.5 1.0 constant_dynamic-slice_fusion.24
  415.4 1.0 constant_dynamic-slice_fusion.17
  416.5 1.0 constant_dynamic-slice_fusion.24
  430.4 1.0 constant_dynamic-slice_fusion.17
  431.5 1.0 constant_dynamic-slice_fusion.24
  452.0 2.1 convert_bitcast_fusion.2
  454.1 2.7 convert_bitcast_fusion
  456.9 16.9 %reduce-scatter.8.cloned.1.call-done = bf16[1,128,512]{2,1,0:T(8,128)(2,1)} async-done(((bf16[1,512,512]{2,1,0:T(8,128)(2,1)}), bf16[1,128,512]{2,1,0:T(8,128)(2,1)}) %reduce-scatter.8.cloned.1.call-update) | async-done | bytes 131088 | tf_op jit(solution)/shard_map/reduce_scatter | solution.py:128
  473.7 22.7 %reduce-scatter.6.cloned.1.call-done = bf16[1,128,512]{2,1,0:T(8,128)(2,1)} async-done(((bf16[1,512,512]{2,1,0:T(8,128)(2,1)}), bf16[1,128,512]{2,1,0:T(8,128)(2,1)}) %reduce-scatter.6.cloned.1.call-update) | async-done | bytes 131088 | tf_op jit(solution)/shard_map/reduce_scatter | solution.py:125
  496.4 38.0 %reduce-scatter.4.cloned.1.call-done = bf16[1,128,512]{2,1,0:T(8,128)(2,1)} async-done(((bf16[1,1024,512]{2,1,0:T(8,128)(2,1)}), bf16[1,128,512]{2,1,0:T(8,128)(2,1)}) %reduce-scatter.4.cloned.1.call-update) | async-done | bytes 131088 | tf_op jit(solution)/shard_map/reduce_scatter | solution.py:121
  (716 shorter events, 234.4 us)
Async XLA Ops:
  7.2 39.8 %all-gather.8.cloned.1.call-start = ((), (), s32[]{:S(2)}) async-start(), calls=%async_computation.5 | async-start | bytes 1179648 | tf_op jit(solution)/shard_map/all_gather | solution.py:41
  8.9 53.9 %all-gather.6.cloned.1.call-start = ((), (), s32[]{:S(2)}) async-start(), calls=%async_computation.4 | async-start | bytes 1179648 | tf_op jit(solution)/shard_map/all_gather | solution.py:40
  10.6 78.2 %all-gather.4.cloned.1.call-start = ((), (), s32[]{:S(2)}) async-start(), calls=%async_computation.3 | async-start | bytes 1179648 | tf_op jit(solution)/shard_map/all_gather | solution.py:39
  12.4 461.4 %reduce-scatter.8.cloned.1.call-start = ((), (), s32[]{:S(2)}) async-start(), calls=%async_computation.8 | async-start | bytes 655360 | tf_op jit(solution)/shard_map/reduce_scatter | solution.py:128
  88.9 2.8 copy-start
  451.9 44.5 %reduce-scatter.6.cloned.1.call-start = ((), (), s32[]{:S(2)}) async-start(), calls=%async_computation.7 | async-start | bytes 655360 | tf_op jit(solution)/shard_map/reduce_scatter | solution.py:125
  454.1 80.3 %reduce-scatter.4.cloned.1.call-start = ((), (), s32[]{:S(2)}) async-start(), calls=%async_computation.6 | async-start | bytes 1179648 | tf_op jit(solution)/shard_map/reduce_scatter | solution.py:121
Sparse Core Ops, SparseCore 0:
  10.4 26.2 all-gather.7
  39.2 23.5 all-gather.5
  65.3 23.5 all-gather.3
  452.1 21.6 reduce-scatter.7
  476.4 19.9 reduce-scatter.5
  500.0 34.3 reduce-scatter.3
where the time goes:
time: 547 us; the launch traced here: 541 us
  local copies, waits for them, and re-layouts  251 us (46%)
  waiting for transfers between devices  117 us (21%)
  loops' own time  81.7 us (15%)
  blocking collectives  32.5 us (6%)
  matrix products  32 us (6%)
  between operations  14.1 us (3%)
  other arithmetic  12.5 us (2%)
    another operation x1, loops' own time, body(): grad_q, grad_k, grad_v = lax.fori_loop(0, limit, one_tile, start_sums)  81.7 us
    dynamic_slice x144, local copies, waits for them, and re-layouts, add_rows(): current = lax.dynamic_slice_in_dim(total, start, piece.shape[0], 0)  56.2 us
    dynamic_update_slice x120, local copies, waits for them, and re-layouts, add_rows(): return lax.dynamic_update_slice_in_dim(total, current + piece, start, 0)  44.3 us
    reduce_scatter x1, waiting for transfers between devices, body(): lax.psum_scatter(grad_q[None].astype(jnp.bfloat16), 'col', scatter_dimens...  38 us
    all_gather x1, waiting for transfers between devices, body(): lax.all_gather(queries, 'col', axis=1, tiled=True)  23.9 us
    reduce_scatter x1, waiting for transfers between devices, body(): lax.psum_scatter(grad_k[None].astype(jnp.bfloat16), 'row', scatter_dimens...  22.7 us
    dynamic_slice x24, local copies, waits for them, and re-layouts, tile_core(): lax.dynamic_slice_in_dim(query_block, q_start, tile_size, 0)  22.1 us
    dynamic_slice x24, local copies, waits for them, and re-layouts, tile_core(): lax.dynamic_slice_in_dim(value_block, k_start, tile_size, 0)  22.1 us
  transfers between devices with their start and end apart: 6, of which 5 were waited for; matrix products, arithmetic and copies ran while one was open for 2% of the time, Pallas kernels for 0%

commit v1 on v0

v1 whole, which is shorter than its diff:
```python
import functools

import jax
import jax.numpy as jnp
import numpy as np
from jax import lax
from jax.experimental import pallas as pl
from jax.experimental.pallas import tpu as pltpu
from jax.sharding import Mesh
from jax.sharding import PartitionSpec as P

F32 = jnp.float32
BF16 = jnp.bfloat16
LANES = 128
PAD = 16
LOG2E = 1.4426950408889634
NT = (((1,), (1,)), ((), ()))
NN = (((1,), (0,)), ((), ()))
PARAMS = pltpu.CompilerParams(vmem_limit_bytes=40 * 1024 * 1024)
VMEM = pl.BlockSpec(memory_space=pltpu.VMEM)
SMEM = pl.BlockSpec(memory_space=pltpu.SMEM)


def pack_kernel(heads, q_ref, g_ref, o_ref, k_ref, v_ref, qg_ref, kv_ref):
    chips, cores, _, half = qg_ref.shape
    rows = q_ref.shape[1]
    krows = k_ref.shape[1]
    width = q_ref.shape[2]
    head_dim = width // heads
    q, g, k, v = q_ref[0], g_ref[0], k_ref[0], v_ref[0]
    product = g.astype(F32) * o_ref[0].astype(F32)
    feature = lax.broadcasted_iota(jnp.int32, (2 * PAD, width), 1)
    head = lax.broadcasted_iota(jnp.int32, (2 * PAD, width), 0)
    local = heads // cores
    wanted = jnp.where(head % PAD < local, head // PAD * local + head % PAD, -1)
    pick = (feature // head_dim == wanted).astype(F32)
    delta = lax.dot_general(
        pick, product, NT, precision=lax.Precision.HIGHEST, preferred_element_type=F32
    ).astype(BF16)
    for core in range(cores):
        lanes = slice(core * half, (core + 1) * half)
        for chip in range(chips):
            qg_ref[chip, core, :rows] = q[:, lanes]
            qg_ref[chip, core, rows : 2 * rows] = g[:, lanes]
            qg_ref[chip, core, 2 * rows :, :rows] = delta[core * PAD : (core + 1) * PAD]
            qg_ref[chip, core, 2 * rows :, rows:] = jnp.zeros((PAD, half - rows), BF16)
        for row in range(kv_ref.shape[0]):
            kv_ref[row, core, :krows] = k[:, lanes]
            kv_ref[row, core, krows:] = v[:, lanes]


def pair_kernel(
    head_dim, tile, capacity,
    info_ref, qg_ref, kv_ref, own_ref, sib_ref, lse_ref,
    dq_ref, dkv_ref,
    q_scr, g_scr, k2t_scr, lse_scr, delta_scr, dqt_scr, dk_scr, dv_scr,
):
    sources, _, half = qg_ref.shape
    rows = (qg_ref.shape[1] - PAD) // 2
    row_count, cores, krows2, _ = kv_ref.shape
    krows = krows2 // 2
    per = tile // krows
    key_tiles = row_count // per
    pairs = half // LANES
    local = half // head_dim
    scaling = float(head_dim) ** -0.5
    core = info_ref[2 * (capacity + 1)]

    lse_scr[...] = lse_ref[core] * LOG2E
    for source in range(sources):
        span = slice(source * rows, (source + 1) * rows)
        q_scr[span] = qg_ref[source, :rows]
        g_scr[span] = qg_ref[source, rows : 2 * rows]
        delta_scr[:, span] = qg_ref[source, 2 * rows :, :rows].astype(F32)
    low_lane = lax.broadcasted_iota(jnp.int32, (tile, LANES), 1) < head_dim
    low_row = lax.broadcasted_iota(jnp.int32, (LANES, tile), 0) < head_dim
    zero = jnp.zeros((tile, LANES), BF16)
    zero_t = jnp.zeros((LANES, tile), BF16)
    bit = lax.shift_left(
        jnp.int32(1), lax.broadcasted_iota(jnp.int32, (tile // 16, 16, tile), 1)
    ).reshape(tile, tile)

    def key_part(w, block, part):
        piece = kv_ref[pl.ds(w * per, per), block, part * krows : (part + 1) * krows]
        return piece.reshape(tile, half)

    for block in range(cores):
        for w in range(key_tiles):
            flipped = key_part(w, block, 0).T
            for pair in range(pairs):
                part = flipped[pair * LANES : (pair + 1) * LANES]
                k2t_scr[block * key_tiles + w, pair] = jnp.concatenate(
                    [jnp.where(low_row, part, zero_t), jnp.where(low_row, zero_t, part)], axis=1
                )
    dqt_scr[...] = jnp.zeros_like(dqt_scr)
    dk_scr[...] = jnp.zeros_like(dk_scr)
    dv_scr[...] = jnp.zeros_like(dv_scr)

    def twice(piece):
        return jnp.concatenate(
            [jnp.where(low_lane, piece, zero), jnp.where(low_lane, zero, piece)], axis=0
        )

    for which, bits_ref in enumerate((own_ref, sib_ref)):
        base = which * (capacity + 1)
        block = core if which == 0 else 1 - core

        def one_tile(entry, _, base=base, block=block, bits_ref=bits_ref):
            slot = info_ref[base + entry]
            u = slot // key_tiles
            w = slot % key_tiles
            kidx = block * key_tiles + w
            qrow = pl.multiple_of(u * tile, tile)
            words = bits_ref[entry]
            words = jnp.broadcast_to(words[:, None, :], (tile // 16, 16, tile)).reshape(tile, tile)
            edge = (words & bit) != 0
            k_tile = key_part(w, block, 0)
            v_tile = key_part(w, block, 1)
            q_tile = q_scr[pl.ds(qrow, tile)]
            g_tile = g_scr[pl.ds(qrow, tile)]
            lse_tile = lse_scr[:, pl.ds(qrow, tile)]
            delta_tile = delta_scr[:, pl.ds(qrow, tile)]
            for pair in range(pairs):
                lanes = slice(pair * LANES, (pair + 1) * LANES)
                q2 = twice(q_tile[:, lanes])
                g2 = twice(g_tile[:, lanes])
                scores = lax.dot_general(k_tile[:, lanes], q2, NT, preferred_element_type=F32)
                grad_prob = lax.dot_general(v_tile[:, lanes], g2, NT, preferred_element_type=F32)
                probs, grads = [], []
                for side in range(2):
                    h = 2 * pair + side
                    s = scores[:, side * tile : (side + 1) * tile]
                    gp = grad_prob[:, side * tile : (side + 1) * tile]
                    p = jnp.exp2(s * (scaling * LOG2E) - lse_tile[h : h + 1])
                    p = jnp.where(edge, p, 0.0)
                    ds = p * (gp - delta_tile[h : h + 1])
                    probs.append(p.astype(BF16))
                    grads.append(ds.astype(BF16))
                p2 = jnp.concatenate(probs, axis=1)
                ds2 = jnp.concatenate(grads, axis=1)
                dv_scr[kidx, :, lanes] += lax.dot_general(p2, g2, NN, preferred_element_type=F32)
                dk_scr[kidx, :, lanes] += lax.dot_general(ds2, q2, NN, preferred_element_type=F32)
                dqt_scr[u, lanes] += lax.dot_general(
                    k2t_scr[kidx, pair], jnp.concatenate(grads, axis=0), NN,
                    preferred_element_type=F32,
                )
            return 0

        lax.fori_loop(0, info_ref[base + capacity], one_tile, 0)

    flat = []
    for u in range(dqt_scr.shape[0]):
        flat.append((dqt_scr[u] * scaling).T.astype(BF16))
    per_q = tile // rows
    for source in range(sources):
        inner = source % per_q
        dq_ref[source] = flat[source // per_q][inner * rows : (inner + 1) * rows]
    for block in range(cores):
        for w in range(key_tiles):
            dk = (dk_scr[block * key_tiles + w] * scaling).astype(BF16)
            dv = dv_scr[block * key_tiles + w].astype(BF16)
            for inner in range(per):
                span = slice(inner * krows, (inner + 1) * krows)
                dkv_ref[w * per + inner, block, :krows] = dk[span]
                dkv_ref[w * per + inner, block, krows:] = dv[span]


def sum_kernel(dq_ref, dkv_ref, dq_out, dk_out, dv_out):
    chips, cores, _, half = dq_ref.shape
    row_count = dkv_ref.shape[0]
    krows = dkv_ref.shape[2] // 2
    for core in range(cores):
        lanes = slice(core * half, (core + 1) * half)
        total = dq_ref[0, core].astype(F32)
        for chip in range(1, chips):
            total += dq_ref[chip, core].astype(F32)
        dq_out[0, :, lanes] = total.astype(BF16)
        total = dkv_ref[0, core].astype(F32)
        for row in range(1, row_count):
            total += dkv_ref[row, core].astype(F32)
        total = total.astype(BF16)
        dk_out[0, :, lanes] = total[:krows]
        dv_out[0, :, lanes] = total[krows:]


def body(sizes, queries, keys, values, outputs, grad_out, lse, tile_slot, tile_live, tile_bits):
    row_count, chips, cores = sizes
    heads = lse.shape[1]
    width = queries.shape[2]
    half = width // cores
    head_dim = width // heads
    local = heads // cores
    tile = tile_bits.shape[4]
    capacity = tile_slot.shape[2]
    rows = queries.shape[1]
    krows = keys.shape[1]
    sources = chips * cores
    query_count = lse.shape[2]
    key_tiles = row_count * krows // tile
    swap = [(core, cores - 1 - core) for core in range(cores)]

    info = jnp.concatenate([tile_slot[0, 0], tile_live[0]])
    info_sib = lax.ppermute(info, "core", swap)
    bits = tile_bits[0, 0]
    bits_sib = lax.ppermute(bits, "core", swap)
    info = jnp.concatenate([info, info_sib, lax.axis_index("core")[None].astype(jnp.int32)])

    qg, kv = pl.pallas_call(
        functools.partial(pack_kernel, heads),
        out_shape=(
            jax.ShapeDtypeStruct((chips, cores, 2 * rows + PAD, half), BF16),
            jax.ShapeDtypeStruct((row_count, cores, 2 * krows, half), BF16),
        ),
        in_specs=[VMEM] * 5,
        out_specs=(VMEM, VMEM),
        compiler_params=PARAMS,
        name="pack",
    )(queries, grad_out, outputs, keys, values)
    qg = qg.reshape(sources, 2 * rows + PAD, half)
    kv = kv.reshape(row_count * cores, 2 * krows, half)
    kv = lax.all_to_all(kv, ("row", "core"), 0, 0, tiled=True)
    qg = lax.all_to_all(qg, ("chip", "core"), 0, 0, tiled=True)
    kv = kv.reshape(row_count, cores, 2 * krows, half)

    dq, dkv = pl.pallas_call(
        functools.partial(pair_kernel, head_dim, tile, capacity),
        out_shape=(
            jax.ShapeDtypeStruct((sources, rows, half), BF16),
            jax.ShapeDtypeStruct((row_count, cores, 2 * krows, half), BF16),
        ),
        in_specs=[SMEM] + [VMEM] * 5,
        out_specs=(VMEM, VMEM),
        scratch_shapes=[
            pltpu.VMEM((query_count, half), BF16),
            pltpu.VMEM((query_count, half), BF16),
            pltpu.VMEM((cores * key_tiles, half // LANES, LANES, 2 * tile), BF16),
            pltpu.VMEM((local, query_count), F32),
            pltpu.VMEM((PAD, query_count), F32),
            pltpu.VMEM((query_count // tile, half, tile), F32),
            pltpu.VMEM((cores * key_tiles, tile, half), F32),
            pltpu.VMEM((cores * key_tiles, tile, half), F32),
        ],
        compiler_params=PARAMS,
        name="pair",
    )(info, qg, kv, bits, bits_sib, lse.reshape(cores, local, query_count))

    dkv = lax.all_to_all(
        dkv.reshape(row_count * cores, 2 * krows, half), ("row", "core"), 0, 0, tiled=True
    )
    dq = lax.all_to_all(dq, ("chip", "core"), 0, 0, tiled=True)
    return pl.pallas_call(
        sum_kernel,
        out_shape=(
            jax.ShapeDtypeStruct((1, rows, width), BF16),
            jax.ShapeDtypeStruct((1, krows, width), BF16),
            jax.ShapeDtypeStruct((1, krows, width), BF16),
        ),
        in_specs=[VMEM] * 2,
        out_specs=(VMEM, VMEM, VMEM),
        compiler_params=PARAMS,
        name="total",
    )(
        dq.reshape(chips, cores, rows, half),
        dkv.reshape(row_count, cores, 2 * krows, half),
    )


def solution(mesh):
    row_count, columns = mesh.devices.shape
    cores = 2
    chips = columns // cores
    fine = Mesh(mesh.devices.reshape(row_count, chips, cores), ("row", "chip", "core"))
    col = ("chip", "core")
    in_specs = (
        P("row", col, None),
        P(col, "row", None),
        P(col, "row", None),
        P("row", col, None),
        P("row", col, None),
        P("row", None, None),
        P("row", col, None),
        P("row", col),
        P("row", col, None, None, None),
    )
    out_specs = (P("row", col, None), P(col, "row", None), P(col, "row", None))
    return jax.shard_map(
        functools.partial(body, (row_count, chips, cores)),
        mesh=fine, in_specs=in_specs, out_specs=out_specs, check_vma=False,
    )
```

time: 547 us -> 119 us (0.22)
  local copies, waits for them, and re-layouts: 251 us -> 4.54 us
  waiting for transfers between devices: 117 us -> 25.2 us
  loops' own time: 81.7 us -> 0 us
  blocking collectives: 32.5 us -> 72.7 us
  matrix products: 32 us -> 0 us
  between operations: 14.1 us -> 1.32 us
  other arithmetic: 12.5 us -> 0.15 us
  Pallas kernels: 0 us -> 7.85 us
    dynamic_slice x288 -> x0, local copies, waits for them, and re-layouts: 175 us -> none  [the longest x144 56.2 us: add_rows(): current = lax.dynamic_slice_in_dim(total, start, piece.shape[0], 0)]
    another operation x1 -> x0, loops' own time: 81.7 us -> none  [body(): grad_q, grad_k, grad_v = lax.fori_loop(0, limit, one_tile, start_sums)]
    reduce_scatter x3 -> x0, waiting for transfers between devices: 77.5 us -> none  [the longest x1 38 us: body(): lax.psum_scatter(grad_q[None].astype(jnp.bfloat16), 'col', scatter_dimens...]
    all_to_all x0 -> x3, blocking collectives: none -> 72.7 us  [the longest x1 30.8 us: body(): lax.all_to_all(dkv.reshape(row_count * cores, 2 * krows, half), ('row', '...]
    dynamic_update_slice x120 -> x0, local copies, waits for them, and re-layouts: 44.3 us -> none  [add_rows(): return lax.dynamic_update_slice_in_dim(total, current + piece, start, 0)]
    all_gather x3 -> x0, waiting for transfers between devices: 39.7 us -> none  [the longest x1 23.9 us: body(): lax.all_gather(queries, 'col', axis=1, tiled=True)]
    all_gather x2 -> x0, blocking collectives: 32.5 us -> none  [the longest x1 17.1 us: body(): lax.all_gather(values, 'row', axis=1, tiled=True)]
    dot_general x120 -> x0, matrix products: 32 us -> none  [the longest x24 8.03 us: tile_core(): jnp.einsum('ihd,jhd->hij', q_tile, k_tile, preferred_element_type=jnp.flo...]
  transfers between devices with their start and end apart: 6 -> 3, of which waited for: 5 -> 3; matrix products, arithmetic and copies ran while one was open for 2% -> 0% of each run, Pallas kernels for 0% -> 0%
where the time goes in v1:
time: 119 us; the launch traced here: 117 us
  blocking collectives  72.7 us (61%)
  waiting for transfers between devices  25.2 us (21%)
  Pallas kernels  7.85 us (7%)
  starting transfers between devices  5.61 us (5%)
  local copies, waits for them, and re-layouts  4.54 us (4%)
  between operations  1.32 us (1%)
    all_to_all x1, blocking collectives, body(): lax.all_to_all(dkv.reshape(row_count * cores, 2 * krows, half), ('row', '...  30.8 us
    all_to_all x1, waiting for transfers between devices, body(): kv = lax.all_to_all(kv, ('row', 'core'), 0, 0, tiled=True)  24 us
    all_to_all x1, blocking collectives, body(): qg = lax.all_to_all(qg, ('chip', 'core'), 0, 0, tiled=True)  21 us
    all_to_all x1, blocking collectives, body(): dq = lax.all_to_all(dq, ('chip', 'core'), 0, 0, tiled=True)  20.8 us
    pallas_call x1, Pallas kernels, body(): pl.pallas_call(functools.partial(pair_kernel, head_dim, tile, capacity),...  5.68 us
    all_to_all x1, starting transfers between devices, body(): kv = lax.all_to_all(kv, ('row', 'core'), 0, 0, tiled=True)  5.01 us
    unnamed x16, local copies, waits for them, and re-layouts  4.52 us
  transfers between devices with their start and end apart: 3, of which 3 were waited for; matrix products, arithmetic and copies ran while one was open for 0% of the time, Pallas kernels for 0%

profile of v1, /device:TPU:0, one launch (start us, length us, event | category | flops | bytes accessed | tf_op | source)
XLA Modules:
  0.0 117.3 jit_solution(1550749888764882539)
XLA Ops:
  0.6 0.0 copy-start
  0.6 0.9 copy-done
  1.5 0.0 copy-start.1
  1.5 0.9 copy-done.1
  2.4 0.0 copy-start.2
  2.4 0.9 copy-done.2
  3.3 0.0 copy-start.3
  3.3 0.9 copy-done.3
  4.3 0.0 copy-start.4
  4.3 0.9 copy-done.4
  5.2 1.3 %pack.1 = (bf16[4,2,272,256]{3,2,1,0:T(8,128)(2,1)S(1)}, bf16[4,2,256,256]{3,2,1,0:T(8,128)(2,1)}) custom-call(bf16[1,128,512]{2,1,0:T(8,128)(2,1)S(1)} %copy-done, bf16[1,128,512]{2,1,0:T(8,128)(2,1)S(1)} %copy-done.1, bf16[1,128,512]{2,1,0:T(8,128)(2,1)S(1)} %copy-done.2, bf16[1,128,512]{2,1,0:T(8,128)(2,1)S(1)} %copy-done.3, ...), custom_call_target="tpu_custom_call" | custom-call | tf_op jit(solution)/shard_map/pack/pallas_call | solution.py:208
  6.5 21.0 %all_to_all.20.qg_ref = bf16[8,272,256]{2,1,0:T(8,128)(2,1)S(1)} all-to-all(bf16[8,272,256]{2,1,0:T(8,128)(2,1)S(1)} %bitcast.15), channel_id=1, replica_groups=mesh['row'=4,'chip'=4,'core'=2] {'chip','core'}, dimensions={0} | all-to-all | bytes 2228224 | tf_op jit(solution)/shard_map/all_to_all | solution.py:222
  27.5 0.0 copy-start.7
  27.5 0.0 copy-start.5
  27.5 0.0 copy-start.6
  27.5 5.0 %all-to-all-start.1 = ((bf16[8,256,256]{2,1,0:T(8,128)(2,1)}), bf16[8,256,256]{2,1,0:T(8,128)(2,1)S(1)}, u32[]{:S(2)}, u32[]{:S(2)}) async-start(bf16[8,256,256]{2,1,0:T(8,128)(2,1)} %bitcast.4), calls=%async_computation.1 | async-start | bytes 2097152 | tf_op jit(solution)/shard_map/all_to_all | solution.py:221
  33.1 0.0 copy-done.7
  33.2 0.1 pad_add_fusion
  33.2 0.5 collective-permute-start
  33.7 0.0 copy-done.5
  33.8 0.1 collective-permute-start.1
  33.8 0.0 copy-done.6
  33.9 0.7 collective-permute-done
  34.6 0.1 pad_add_fusion.1.info_ref
  34.6 0.4 collective-permute-done.1.sib_ref
  35.1 24.0 %all-to-all-done.1 = bf16[8,256,256]{2,1,0:T(8,128)(2,1)S(1)} async-done(((bf16[8,256,256]{2,1,0:T(8,128)(2,1)}), bf16[8,256,256]{2,1,0:T(8,128)(2,1)S(1)}, u32[]{:S(2)}, u32[]{:S(2)}) %all-to-all-start.1) | async-done | bytes 1048608 | tf_op jit(solution)/shard_map/all_to_all | solution.py:221
  59.1 5.7 %pair.1 = (bf16[8,128,256]{2,1,0:T(8,128)(2,1)S(1)}, bf16[4,2,256,256]{3,2,1,0:T(8,128)(2,1)S(1)}) custom-call(s32[51]{0:T(128)S(1)} %pad_add_fusion.1.info_ref, bf16[8,272,256]{2,1,0:T(8,128)(2,1)S(1)} %all_to_all.20.qg_ref, bf16[4,2,256,256]{3,2,1,0:T(8,128)(2,1)S(1)} %bitcast.13, s32[24,8,128]{2,1,0:T(8,128)S(1)} %bitcast.18, ...), custom_call_target="tpu_custom_call" | custom-call | tf_op jit(solution)/shard_map/pair/pallas_call | solution.py:225
  64.8 20.8 %all_to_all.21 = bf16[8,128,256]{2,1,0:T(8,128)(2,1)S(1)} all-to-all(bf16[8,128,256]{2,1,0:T(8,128)(2,1)S(1)} %get-tuple-element.9), channel_id=1, replica_groups=mesh['row'=4,'chip'=4,'core'=2] {'chip','core'}, dimensions={0} | all-to-all | bytes 1048576 | tf_op jit(solution)/shard_map/all_to_all | solution.py:250
  85.6 30.8 %all_to_all.22 = bf16[8,256,256]{2,1,0:T(8,128)(2,1)S(1)} all-to-all(bf16[8,256,256]{2,1,0:T(8,128)(2,1)S(1)} %bitcast.16), channel_id=1, replica_groups=mesh['row'=4,'chip'=4,'core'=2] {'row','core'}, dimensions={0} | all-to-all | bytes 2097152 | tf_op jit(solution)/shard_map/all_to_all | solution.py:247
  116.4 0.9 total.1
  (1 shorter events, 0.0 us)
Async XLA Ops:
  0.6 0.9 copy-start
  1.5 0.9 copy-start.1
  2.4 0.9 copy-start.2
  3.3 0.9 copy-start.3
  4.3 0.9 copy-start.4
  27.5 5.7 %copy-start.7 = (s32[1,1,24]{2,1,0:T(1,128)S(1)}, s32[1,1,24]{2,1,0:T(1,128)}, u32[]{:S(2)}) copy-start(s32[1,1,24]{2,1,0:T(1,128)} %param.15) | copy-start | bytes 292
  27.5 6.3 %copy-start.5 = (s32[1,1,24,8,128]{4,3,2,1,0:T(8,128)S(1)}, s32[1,1,24,8,128]{4,3,2,1,0:T(8,128)}, u32[]{:S(2)}) copy-start(s32[1,1,24,8,128]{4,3,2,1,0:T(8,128)} %param.17) | copy-start | bytes 294916
  27.5 6.4 %copy-start.6 = (f32[1,8,1024]{2,1,0:T(8,128)S(1)}, f32[1,8,1024]{2,1,0:T(8,128)}, u32[]{:S(2)}) copy-start(f32[1,8,1024]{2,1,0:T(8,128)} %param.14) | copy-start | bytes 98308
  27.5 31.6 %all-to-all-start.1 = ((bf16[8,256,256]{2,1,0:T(8,128)(2,1)}), bf16[8,256,256]{2,1,0:T(8,128)(2,1)S(1)}, u32[]{:S(2)}, u32[]{:S(2)}) async-start(bf16[8,256,256]{2,1,0:T(8,128)(2,1)} %bitcast.4), calls=%async_computation.1 | async-start | bytes 2097152 | tf_op jit(solution)/shard_map/all_to_all | solution.py:221
  33.2 1.3 %collective-permute-start = (s32[25]{0:T(128)S(1)}, s32[25]{0:T(128)S(1)}, u32[]{:S(2)}, u32[]{:S(2)}) collective-permute-start(s32[25]{0:T(128)S(1)} %pad_add_fusion), channel_id=1, source_target_pairs={{0,1},{1,0},{2,3},{3,2},{4,5},{5,4},{6,7},{7,6},{8,9},{9,8},{10,11... | collective-permute-start | bytes 308 | tf_op jit(solution)/shard_map/ppermute | solution.py:203
  33.8 1.3 %collective-permute-start.1 = (s32[24,8,128]{2,1,0:T(8,128)S(1)}, s32[24,8,128]{2,1,0:T(8,128)S(1)}, u32[]{:S(2)}, u32[]{:S(2)}) collective-permute-start(s32[24,8,128]{2,1,0:T(8,128)S(1)} %bitcast.17), channel_id=1, source_target_pairs={{0,1},{1,0},{2,3},{3,2},{4,5},{5,4},{6,7},{7,6},{8,9},{9,8},{10,11... | collective-permute-start | bytes 294920 | tf_op jit(solution)/shard_map/ppermute | solution.py:205
